TPU v7x, 256 devices: a whole 4x4x8 slice. The times are simulated.
256 devices in a mesh: row: 8 (over x, core), col: 32 (over z, y).
Axes of the slice: x: 4, y: 4, z: 8, core: 2. Of those that a mesh axis runs over, the one named last changes fastest.
Arguments:
- fields: bfloat16 [4, 64, 768, 1536], P(None, 'row', 'col'), may hold values from -1.5 to 3, as said below
- block_points: int32 [8, 32, 48, 256], P('row', 'col'), may hold values from 0 to 24575
- sample_weight: bfloat16 [8, 32, 48, 256], P('row', 'col'), may hold values from 0.099609375 to 1
- block_turbine: int32 [8, 32, 48], P('row'), may hold values from 0 to 399, as said below
- block_count: int32 [8, 32], P('row'), may hold values from 36 to 48, as said below
Outputs:
- tendency: bfloat16 [4, 64, 768, 1536], P(None, 'row', 'col')
- thrust: float32 [8, 32, 48, 256], P('row', 'col')
Inputs may be any that keep to these rules, and one draw needn't show every extreme that they name: `block_turbine`: entry [r, c, :] lists the turbines of the blocks of the device at row index r and col index c; turbine t belongs to owner col index t mod 32. Of one device's 48 blocks at most 3 have turbines of one owner col index, and in every row index some owner col index gets exactly 3 blocks from every device of that row index. `block_count`: A device's live blocks are its first ones; some device has all of them live. `fields`: field 0 is the streamwise velocity.
All inputs are finite; a program needn't handle non-finite values.
Results may differ from a plain program's by a relative error of at most 0.0036.
Values may be sent and summed in bfloat16 or wider, within the bound.
A program may use at most 128 MiB of HBM per device.

v0:
```python
import jax
import jax.numpy as jnp
from jax import lax
from jax.sharding import PartitionSpec as P

NY = 768
TURBINES = 400


CT_HALF = 2.0 / 3.0
BUOYANCY = 0.3
HIGHEST = lax.Precision.HIGHEST


def spectral_table(length):
    counter = jnp.arange(length, dtype=jnp.int32)
    offset = (counter[:, None] - counter[None, :]) % length
    phase_angle = offset.astype(jnp.float32) * (jnp.pi / length)
    parity = 1.0 - 2.0 * (offset % 2).astype(jnp.float32)
    sine_safe = jnp.where(offset == 0, 1.0, jnp.sin(phase_angle))
    entries = -(jnp.pi / length) * parity * jnp.cos(phase_angle) / sine_safe
    return jnp.where(offset == 0, 0.0, entries).astype(jnp.bfloat16)


def earlier_equal(targets):
    length = targets.shape[-1]
    counter = jnp.arange(length, dtype=jnp.int32)
    before = counter[None, :] < counter[:, None]
    matching = targets[..., :, None] == targets[..., None, :]
    return jnp.sum(matching & before, axis=-1)


def per_device(fields, block_points, sample_weight, block_turbine, block_count):
    columns = lax.axis_size("col")
    here_col = lax.axis_index("col")
    levels = fields.shape[1]
    local_rows = fields.shape[2]
    full_width = fields.shape[3]
    table_x = spectral_table(full_width)
    table_y = spectral_table(NY)
    slope_x = lax.dot_general(
        fields, table_x, (((3,), (0,)), ((), ())), preferred_element_type=jnp.float32
    )
    pencil = lax.all_to_all(fields, "col", split_axis=3, concat_axis=2, tiled=True)
    slope_y = lax.dot_general(
        pencil, table_y, (((2,), (0,)), ((), ())), preferred_element_type=jnp.float32
    )
    across = jnp.swapaxes(pencil[1], 1, 2).astype(jnp.float32)
    carried = (across[None] * slope_y).astype(jnp.bfloat16)
    returned = lax.all_to_all(carried, "col", split_axis=3, concat_axis=2, tiled=True)
    term_y = jnp.swapaxes(returned, 2, 3).astype(jnp.float32)
    blocks = block_points.shape[2]
    samples = block_points.shape[3]
    capacity = max(2, 2 * blocks // columns)
    locations = block_points[0, 0]
    lines_all = levels * local_rows
    rotor_lines = min(lines_all, 16)
    plane_lines = fields[0].reshape(lines_all, full_width)[:rotor_lines]
    group = max([d for d in range(1, 9) if blocks % d == 0])
    grouped_points = locations.reshape(blocks // group, group * samples)
    line_ids = jnp.arange(rotor_lines, dtype=jnp.int32)
    column_ids = jnp.arange(full_width, dtype=jnp.int32)

    def pick_values(points):
        line_hot = (points[:, None] // full_width == line_ids[None, :]).astype(jnp.bfloat16)
        picked_lines = jnp.dot(line_hot, plane_lines, preferred_element_type=jnp.float32)
        column_hot = points[:, None] % full_width == column_ids[None, :]
        return jnp.sum(jnp.where(column_hot, picked_lines, 0.0), -1)

    sampled = lax.map(pick_values, grouped_points).reshape(blocks, samples)
    turbines_here = lax.dynamic_index_in_dim(block_turbine[0], here_col, 0, keepdims=False)
    count_here = lax.dynamic_index_in_dim(block_count[0], here_col, 0, keepdims=False)
    block_ids = jnp.arange(blocks, dtype=jnp.int32)
    active = (block_ids < count_here).astype(jnp.float32)
    weight = sample_weight[0, 0].astype(jnp.float32) * active[:, None]
    turbine_ids = jnp.arange(TURBINES, dtype=jnp.int32)
    target = turbines_here % columns
    position = earlier_equal(target)
    slot_ids = jnp.arange(columns * capacity, dtype=jnp.int32)
    placement = (slot_ids[:, None] == (target * capacity + position)[None, :]).astype(jnp.float32)
    outgoing = jnp.stack([sampled * active[:, None], weight])
    packed = jnp.einsum("kb,fbs->fks", placement, outgoing, precision=HIGHEST).astype(jnp.bfloat16)
    arrived = lax.all_to_all(packed, "col", split_axis=1, concat_axis=1, tiled=True).astype(
        jnp.float32
    )
    every_turbine = block_turbine[0]
    every_target = every_turbine % columns
    every_position = earlier_equal(every_target)
    every_active = block_ids[None, :] < block_count[0][:, None]
    slot_range = jnp.arange(capacity, dtype=jnp.int32)
    chosen = (
        (every_target == here_col)[:, None, :]
        & (every_position[:, None, :] == slot_range[None, :, None])
        & every_active[:, None, :]
    )
    belongs = (every_turbine[:, :, None] == turbine_ids[None, None, :]).astype(jnp.float32)
    holdings = jnp.einsum(
        "scb,sbt->sct", chosen.astype(jnp.float32), belongs, precision=HIGHEST
    ).reshape(columns * capacity, TURBINES)
    moments = jnp.stack([jnp.sum(arrived[1] * arrived[0], -1), jnp.sum(arrived[1], -1)], -1)
    partial_value = jnp.dot(holdings.T, moments, precision=HIGHEST)
    totals = lax.psum(partial_value, "row")
    looked_up = jnp.dot(holdings, totals, precision=HIGHEST)
    vacant = 1.0 - jnp.sum(holdings, -1)
    disk_speed = looked_up[:, 0] / (looked_up[:, 1] + vacant)
    slot_thrust = -CT_HALF * (disk_speed * jnp.abs(disk_speed))[:, None] * arrived[1]
    thrust_back = lax.all_to_all(slot_thrust, "col", split_axis=0, concat_axis=0, tiled=True)
    thrust = jnp.dot(placement.T, thrust_back, precision=HIGHEST)
    grouped_thrust = thrust.reshape(blocks // group, group * samples)

    def spread_values(total, pair):
        points, values = pair
        line_hot = (points[:, None] // full_width == line_ids[None, :]).astype(jnp.float32)
        column_values = jnp.where(
            points[:, None] % full_width == column_ids[None, :], values[:, None], 0.0
        )
        added = lax.dot_general(
            line_hot, column_values, (((0,), (0,)), ((), ())), precision=HIGHEST
        )
        return (total + added, None)

    rotor_force, unused = lax.scan(
        spread_values,
        jnp.zeros((rotor_lines, full_width), jnp.float32),
        (grouped_points, grouped_thrust),
    )
    rest_lines = jnp.zeros((lines_all - rotor_lines, full_width), jnp.float32)
    forcing = jnp.concatenate([rotor_force, rest_lines], 0).reshape(levels, local_rows, full_width)
    speed_field = fields[0].astype(jnp.float32)
    advect = -(speed_field[None] * slope_x) - term_y
    nothing = jnp.zeros((levels, local_rows, full_width), jnp.float32)
    source_terms = jnp.stack([forcing, nothing, BUOYANCY * fields[3].astype(jnp.float32), nothing])
    tendency = (advect + source_terms).astype(jnp.bfloat16)
    return (tendency, thrust[None, None])


def solution(mesh):
    placed = (
        P(None, "row", "col", None),
        P("row", "col", None, None),
        P("row", "col", None, None),
        P("row", None, None),
        P("row", None),
    )
    return jax.shard_map(
        per_device,
        mesh=mesh,
        in_specs=placed,
        out_specs=(P(None, "row", "col", None), P("row", "col", None, None)),
        check_vma=False,
    )
```

profile of v0, /device:TPU:8, one launch (start us, length us, event | category | flops | bytes accessed | tf_op | source)
XLA Modules:
  0.0 401.0 jit_solution(12403995199545525736)
XLA Ops:
  7.3 16.2 %while.26 = (s32[]{:T(128)}, f32[6,2048]{1,0:T(8,128)S(1)}, s32[6,2048]{1,0:T(8,128)S(1)}, bf16[16,1536]{1,0:T(8,128)(2,1)S(1)}, s32[]{:T(128)}, /*index=5*/s32[]{:T(128)}) while((s32[]{:T(128)}, f32[6,2048]{1,0:T(8,128)S(1)}, s32[6,2048]{1,0:T(8,128)S(1)}, bf16[16,1536]{1,0:T(8,128)(2,1)S(1)}, s32[]{:T(128)}, ...), condition=%wide.region_4.5_spmd.clone, body=%wide.region_2.4_spmd.clone.sunk | while | flops 110155776 | bytes 159825 | solution.py:70
  7.5 2.4 select_reduce_fusion.2
  12.9 2.4 select_reduce_fusion.2
  18.3 2.4 select_reduce_fusion.2
  24.8 11.7 %all-to-all-start.2 = ((bf16[2,96,256]{2,0,1:T(2,128)(2,1)}), bf16[2,96,256]{2,0,1:T(2,128)(2,1)S(1)}, u32[]{:S(2)}, u32[]{:S(2)}) async-start(bf16[2,96,256]{2,0,1:T(2,128)(2,1)} %copy.29), calls=%async_computation.2 | async-start | bytes 196608 | tf_op jit(solution)/shard_map/all_to_all | solution.py:83
  38.5 6.8 %all-to-all-done.2 = bf16[2,96,256]{2,0,1:T(2,128)(2,1)S(1)} async-done(((bf16[2,96,256]{2,0,1:T(2,128)(2,1)}), bf16[2,96,256]{2,0,1:T(2,128)(2,1)S(1)}, u32[]{:S(2)}, u32[]{:S(2)}) %all-to-all-start.2) | async-done | bytes 98336 | tf_op jit(solution)/shard_map/all_to_all | solution.py:83
  46.4 13.2 %psum.7 = f32[400,2]{0,1:T(2,128)S(1)} all-reduce(f32[400,2]{0,1:T(2,128)S(1)} %fusion.92), channel_id=1, replica_groups=mesh['row'=8,'col'=32] {'row'}, use_global_device_ids=true, to_apply=%region_7.8 | all-reduce | flops 800 | bytes 6400 | tf_op jit(solution)/shard_map/psum | solution.py:102
  60.8 5.2 %all-to-all-start.3 = ((f32[32,3,256]{2,1,0:T(4,128)}), f32[32,3,256]{2,1,0:T(4,128)S(1)}, u32[]{:S(2)}, u32[]{:S(2)}) async-start(f32[32,3,256]{2,1,0:T(4,128)} %broadcast_multiply_fusion), calls=%async_computation.3 | async-start | bytes 262144 | tf_op jit(solution)/shard_map/all_to_all | solution.py:107
  66.0 17.5 %copy.22 = bf16[4,8,24,1536]{2,1,0,3:T(8,128)(2,1)} copy(bf16[4,8,24,1536]{3,2,1,0:T(8,128)(2,1)S(1)} %copy-done) | data formatting | bytes 4718592 | tf_op args[0]
  83.5 19.2 %reshape.418 = bf16[32,2,18432]{2,1,0:T(2,128)(2,1)} reshape(bf16[1536,4,8,24]{3,2,1,0:T(8,128)(2,1)} %bitcast.106) | data formatting | bytes 4718592
  102.7 10.5 %all-to-all-start = ((bf16[32,2,18432]{2,1,0:T(2,128)(2,1)}), bf16[32,2,18432]{2,1,0:T(2,128)(2,1)S(1)}, u32[]{:S(2)}, u32[]{:S(2)}) async-start(bf16[32,2,18432]{2,1,0:T(2,128)(2,1)} %reshape.418), calls=%async_computation | async-start | bytes 4718592 | tf_op jit(solution)/shard_map/all_to_all | solution.py:44
  115.7 51.1 %all-to-all-done = bf16[32,2,18432]{2,1,0:T(2,128)(2,1)S(1)} async-done(((bf16[32,2,18432]{2,1,0:T(2,128)(2,1)}), bf16[32,2,18432]{2,1,0:T(2,128)(2,1)S(1)}, u32[]{:S(2)}, u32[]{:S(2)}) %all-to-all-start) | async-done | bytes 2359328 | tf_op jit(solution)/shard_map/all_to_all | solution.py:44
  166.8 18.5 %reshape.419 = bf16[1536,4,8,24]{3,2,1,0:T(8,128)(2,1)} reshape(bf16[32,2,18432]{2,1,0:T(2,128)(2,1)S(1)} %all-to-all-done) | data formatting | bytes 4718592
  185.3 16.9 %copy.23 = bf16[4,8,24,32,48]{4,2,3,1,0:T(8,128)(2,1)} copy(bf16[4,8,24,32,48]{2,1,0,4,3:T(8,128)(2,1)} %bitcast.105) | data formatting | bytes 4718592 | tf_op jit(solution)/shard_map/all_to_all | solution.py:44
  206.0 17.3 %fusion.36 = bf16[4,8,48,768]{3,2,1,0:T(8,128)(2,1)S(1)} fusion(f32[8,48,768]{2,1,0:T(8,128)} %copy.24, bf16[4,8,768,48]{3,2,1,0:T(8,128)(2,1)} %bitcast.111), kind=kOutput, calls=%fused_computation.58 | convolution fusion | flops 1831993344 | bytes 5898240 | tf_op jit(solution)/shard_map/dot_general | solution.py:45
  223.4 9.3 %copy.26 = bf16[4,8,48,768]{2,1,0,3:T(8,128)(2,1)} copy(bf16[4,8,48,768]{3,2,1,0:T(8,128)(2,1)S(1)} %fusion.36) | data formatting | bytes 4718592 | tf_op jit(solution)/shard_map/convert_element_type | solution.py:49
  232.7 11.5 %reshape.420 = bf16[32,2,18432]{2,1,0:T(2,128)(2,1)} reshape(bf16[768,4,8,48]{3,2,1,0:T(8,128)(2,1)} %bitcast.108) | data formatting | bytes 4718592
  244.2 6.9 %all-to-all-start.1 = ((bf16[32,2,18432]{2,1,0:T(2,128)(2,1)}), bf16[32,2,18432]{2,1,0:T(2,128)(2,1)S(1)}, u32[]{:S(2)}, u32[]{:S(2)}) async-start(bf16[32,2,18432]{2,1,0:T(2,128)(2,1)} %reshape.420), calls=%async_computation.1 | async-start | bytes 4718592 | tf_op jit(solution)/shard_map/all_to_all | solution.py:50
  251.1 33.3 %while.27 = (s32[]{:T(128)}, f32[16,1536]{1,0:T(8,128)S(1)}, s32[6,2048]{1,0:T(8,128)S(1)}, f32[6,2048]{1,0:T(8,128)S(1)}, s32[]{:T(128)}, /*index=5*/s32[]{:T(128)}) while((s32[]{:T(128)}, f32[16,1536]{1,0:T(8,128)S(1)}, s32[6,2048]{1,0:T(8,128)S(1)}, f32[6,2048]{1,0:T(8,128)S(1)}, s32[]{:T(128)}, /*index=5*/s32[]{:T(128)}) %tuple.83), condition=%wide.region_10.11_spmd.clone, body=%wide.region_9.10_spmd.clone.sunk | while | flops 610377728 | bytes 307291 | solution.py:122
  251.3 5.4 %fusion.136 = f32[16,1536]{1,0:T(8,128)S(1)} fusion(f32[2048]{0:T(1024)S(1)} %bitcast.119, s32[2048]{0:T(1024)S(1)} %get-tuple-element.294, s32[2048]{0:T(1024)S(1)} %get-tuple-element.295, f32[16,1536]{1,0:T(8,128)S(1)} %get-tuple-element.321, pred[]{:T(512)S(6)} %compare.26), kind=kOutput, calls=%fused_computation.21.clone.1 | convolution fusion | flops 610353152 | bytes 221185 | tf_op jit(solution)/shard_map/while/body/eval_jaxpr/dot_general | solution.py:117
  256.8 5.4 %fusion.136 = f32[16,1536]{1,0:T(8,128)S(1)} fusion(f32[2048]{0:T(1024)S(1)} %bitcast.119, s32[2048]{0:T(1024)S(1)} %get-tuple-element.294, s32[2048]{0:T(1024)S(1)} %get-tuple-element.295, f32[16,1536]{1,0:T(8,128)S(1)} %get-tuple-element.321, pred[]{:T(512)S(6)} %compare.26), kind=kOutput, calls=%fused_computation.21.clone.1 | convolution fusion | flops 610353152 | bytes 221185 | tf_op jit(solution)/shard_map/while/body/eval_jaxpr/dot_general | solution.py:117
  262.4 5.4 %fusion.136 = f32[16,1536]{1,0:T(8,128)S(1)} fusion(f32[2048]{0:T(1024)S(1)} %bitcast.119, s32[2048]{0:T(1024)S(1)} %get-tuple-element.294, s32[2048]{0:T(1024)S(1)} %get-tuple-element.295, f32[16,1536]{1,0:T(8,128)S(1)} %get-tuple-element.321, pred[]{:T(512)S(6)} %compare.26), kind=kOutput, calls=%fused_computation.21.clone.1 | convolution fusion | flops 610353152 | bytes 221185 | tf_op jit(solution)/shard_map/while/body/eval_jaxpr/dot_general | solution.py:117
  267.9 5.4 %fusion.136 = f32[16,1536]{1,0:T(8,128)S(1)} fusion(f32[2048]{0:T(1024)S(1)} %bitcast.119, s32[2048]{0:T(1024)S(1)} %get-tuple-element.294, s32[2048]{0:T(1024)S(1)} %get-tuple-element.295, f32[16,1536]{1,0:T(8,128)S(1)} %get-tuple-element.321, pred[]{:T(512)S(6)} %compare.26), kind=kOutput, calls=%fused_computation.21.clone.1 | convolution fusion | flops 610353152 | bytes 221185 | tf_op jit(solution)/shard_map/while/body/eval_jaxpr/dot_general | solution.py:117
  273.4 5.4 %fusion.136 = f32[16,1536]{1,0:T(8,128)S(1)} fusion(f32[2048]{0:T(1024)S(1)} %bitcast.119, s32[2048]{0:T(1024)S(1)} %get-tuple-element.294, s32[2048]{0:T(1024)S(1)} %get-tuple-element.295, f32[16,1536]{1,0:T(8,128)S(1)} %get-tuple-element.321, pred[]{:T(512)S(6)} %compare.26), kind=kOutput, calls=%fused_computation.21.clone.1 | convolution fusion | flops 610353152 | bytes 221185 | tf_op jit(solution)/shard_map/while/body/eval_jaxpr/dot_general | solution.py:117
  279.0 5.4 %fusion.136 = f32[16,1536]{1,0:T(8,128)S(1)} fusion(f32[2048]{0:T(1024)S(1)} %bitcast.119, s32[2048]{0:T(1024)S(1)} %get-tuple-element.294, s32[2048]{0:T(1024)S(1)} %get-tuple-element.295, f32[16,1536]{1,0:T(8,128)S(1)} %get-tuple-element.321, pred[]{:T(512)S(6)} %compare.26), kind=kOutput, calls=%fused_computation.21.clone.1 | convolution fusion | flops 610353152 | bytes 221185 | tf_op jit(solution)/shard_map/while/body/eval_jaxpr/dot_general | solution.py:117
  285.5 19.3 %all-to-all-done.1 = bf16[32,2,18432]{2,1,0:T(2,128)(2,1)S(1)} async-done(((bf16[32,2,18432]{2,1,0:T(2,128)(2,1)}), bf16[32,2,18432]{2,1,0:T(2,128)(2,1)S(1)}, u32[]{:S(2)}, u32[]{:S(2)}) %all-to-all-start.1) | async-done | bytes 2359328 | tf_op jit(solution)/shard_map/all_to_all | solution.py:50
  304.9 7.6 %reshape.421 = bf16[768,4,8,48]{3,2,1,0:T(8,128)(2,1)} reshape(bf16[32,2,18432]{2,1,0:T(2,128)(2,1)S(1)} %all-to-all-done.1) | data formatting | bytes 4718592
  312.5 5.2 %copy.27 = bf16[4,8,48,768]{2,3,1,0:T(8,128)(2,1)S(1)} copy(bf16[4,8,48,768]{2,1,0,3:T(8,128)(2,1)} %bitcast.107) | data formatting | bytes 4718592 | tf_op jit(solution)/shard_map/all_to_all | solution.py:50
  317.7 6.1 %convert_bitcast_fusion = f32[4,8,32,48,24]{3,4,2,1,0:T(8,128)} fusion(bf16[4,8,48,32,24]{2,4,3,1,0:T(8,128)(2,1)S(1)} %bitcast.109), kind=kLoop, calls=%fused_computation.37 | loop fusion | flops 1179648 | bytes 7077888 | tf_op jit(solution)/shard_map/convert_element_type | solution.py:51
  323.8 11.4 %copy.28 = f32[4,8,32,48,24]{3,2,4,1,0:T(8,128)} copy(f32[4,8,32,48,24]{3,4,2,1,0:T(8,128)} %convert_bitcast_fusion) | data formatting | bytes 9437184 | tf_op jit(solution)/shard_map/convert_element_type | solution.py:51
  335.2 13.2 %reshape.403 = f32[4,8,1536,24]{2,3,1,0:T(8,128)} reshape(f32[4,8,32,48,24]{3,2,4,1,0:T(8,128)} %copy.28) | data formatting | bytes 9437184 | tf_op jit(solution)/shard_map/convert_element_type | solution.py:51
  348.5 52.2 %fusion.35 = bf16[4,8,24,1536]{3,2,1,0:T(8,128)(2,1)} fusion(f32[1,8,24,1536]{3,2,1,0:T(8,128)S(1)} %broadcast.377, f32[1,8,24,1536]{3,2,1,0:T(8,128)} %convert_multiply_fusion, f32[1,8,24,1536]{3,2,1,0:T(8,128)} %bitcast.113, f32[4,8,1536,24]{2,3,1,0:T(8,128)} %reshape.403, bf16[4,8,24,1536]{3,2,1,0:T(8,128)(2,1)S(1)} %copy-done.1, ...), kind=kOutput, calls=%fused_computation.55 | convolution fusion | flops 3704094720 | bytes 14155776 | tf_op jit(solution)/shard_map/dot_general | solution.py:41
  (104 shorter events, 29.3 us)
Async XLA Ops:
  7.3 16.3 %copy-start.4 = (bf16[1,1,48,256]{3,2,1,0:T(8,128)(2,1)S(1)}, bf16[1,1,48,256]{3,2,1,0:T(8,128)(2,1)}, u32[]{:S(2)}) copy-start(bf16[1,1,48,256]{3,2,1,0:T(8,128)(2,1)} %param.11) | copy-start | bytes 73732
  7.3 29.2 %copy-start.5 = (s32[1,32,48]{2,1,0:T(8,128)S(1)}, s32[1,32,48]{2,1,0:T(8,128)}, u32[]{:S(2)}) copy-start(s32[1,32,48]{2,1,0:T(8,128)} %param.12) | copy-start | bytes 18436
  7.3 29.2 %copy-start.6 = (s32[1,32]{1,0:T(1,128)S(1)}, s32[1,32]{1,0:T(1,128)}, u32[]{:S(2)}) copy-start(s32[1,32]{1,0:T(1,128)} %param.13) | copy-start | bytes 388
  23.6 42.4 %copy-start = (bf16[4,8,24,1536]{3,2,1,0:T(8,128)(2,1)S(1)}, bf16[4,8,24,1536]{3,2,1,0:T(8,128)(2,1)}, u32[]{:S(2)}) copy-start(bf16[4,8,24,1536]{3,2,1,0:T(8,128)(2,1)} %param.9) | copy-start | bytes 7077892
  24.8 20.5 %all-to-all-start.2 = ((bf16[2,96,256]{2,0,1:T(2,128)(2,1)}), bf16[2,96,256]{2,0,1:T(2,128)(2,1)S(1)}, u32[]{:S(2)}, u32[]{:S(2)}) async-start(bf16[2,96,256]{2,0,1:T(2,128)(2,1)} %copy.29), calls=%async_computation.2 | async-start | bytes 196608 | tf_op jit(solution)/shard_map/all_to_all | solution.py:83
  60.8 41.9 %all-to-all-start.3 = ((f32[32,3,256]{2,1,0:T(4,128)}), f32[32,3,256]{2,1,0:T(4,128)S(1)}, u32[]{:S(2)}, u32[]{:S(2)}) async-start(f32[32,3,256]{2,1,0:T(4,128)} %broadcast_multiply_fusion), calls=%async_computation.3 | async-start | bytes 262144 | tf_op jit(solution)/shard_map/all_to_all | solution.py:107
  102.7 64.1 %all-to-all-start = ((bf16[32,2,18432]{2,1,0:T(2,128)(2,1)}), bf16[32,2,18432]{2,1,0:T(2,128)(2,1)S(1)}, u32[]{:S(2)}, u32[]{:S(2)}) async-start(bf16[32,2,18432]{2,1,0:T(2,128)(2,1)} %reshape.418), calls=%async_computation | async-start | bytes 4718592 | tf_op jit(solution)/shard_map/all_to_all | solution.py:44
  115.6 69.6 %copy-start.3 = (f32[48,256]{1,0:T(8,128)}, f32[48,256]{1,0:T(8,128)S(1)}, u32[]{:S(2)}) copy-start(f32[48,256]{1,0:T(8,128)S(1)} %fusion.86) | copy-start | bytes 147460
  244.2 60.7 %all-to-all-start.1 = ((bf16[32,2,18432]{2,1,0:T(2,128)(2,1)}), bf16[32,2,18432]{2,1,0:T(2,128)(2,1)S(1)}, u32[]{:S(2)}, u32[]{:S(2)}) async-start(bf16[32,2,18432]{2,1,0:T(2,128)(2,1)} %reshape.420), calls=%async_computation.1 | async-start | bytes 4718592 | tf_op jit(solution)/shard_map/all_to_all | solution.py:50
  335.2 13.3 %copy-start.1 = (bf16[4,8,24,1536]{3,2,1,0:T(8,128)(2,1)S(1)}, bf16[4,8,24,1536]{3,2,1,0:T(8,128)(2,1)}, u32[]{:S(2)}) copy-start(bf16[4,8,24,1536]{3,2,1,0:T(8,128)(2,1)} %param.9) | copy-start | bytes 7077892
  335.2 13.4 %copy-start.2 = (f32[8,24,1536]{2,1,0:T(8,128)S(1)}, f32[8,24,1536]{2,1,0:T(8,128)}, u32[]{:S(2)}) copy-start(f32[8,24,1536]{2,1,0:T(8,128)} %get-tuple-element.223) | copy-start | bytes 3538948
where the time goes:
time: 409 us; the launch traced here: 401 us
  local copies, waits for them, and re-layouts  140 us (34%)
  matrix products  118 us (29%)
  waiting for transfers between devices  77.2 us (19%)
  starting transfers between devices  34.3 us (8%)
  other arithmetic  17 us (4%)
  blocking collectives  13.2 us (3%)
    unnamed x19, local copies, waits for them, and re-layouts  74.3 us
    dot_general x1, matrix products, per_device(): lax.dot_general(fields, table_x, (((3,), (0,)), ((), ())), preferred_elem...  52.2 us
    all_to_all x1, waiting for transfers between devices, per_device(): lax.all_to_all(fields, 'col', split_axis=3, concat_axis=2, tiled=True)  51.1 us
    dot_general x6, matrix products, spread_values(): lax.dot_general(line_hot, column_values, (((0,), (0,)), ((), ())), precis...  32.4 us
    convert_element_type x2, local copies, waits for them, and re-layouts, per_device(): term_y = jnp.swapaxes(returned, 2, 3).astype(jnp.float32)  24.6 us
    all_to_all x1, waiting for transfers between devices, per_device(): lax.all_to_all(carried, 'col', split_axis=3, concat_axis=2, tiled=True)  19.3 us
    dot_general x1, matrix products, per_device(): lax.dot_general(pencil, table_y, (((2,), (0,)), ((), ())), preferred_elem...  17.3 us
    all_to_all x1, local copies, waits for them, and re-layouts, per_device(): lax.all_to_all(fields, 'col', split_axis=3, concat_axis=2, tiled=True)  16.9 us
  transfers between devices with their start and end apart: 4, of which 3 were waited for; matrix products, arithmetic and copies ran while one was open for 19% of the time, Pallas kernels for 0%

commit v1 on v0

v1 whole, which is shorter than its diff:
```python
import functools

import jax
import jax.numpy as jnp
import ml_dtypes
import numpy as np
from jax import lax
from jax.experimental import pallas as pl
from jax.experimental.pallas import tpu as pltpu
from jax.sharding import PartitionSpec as P

MESH = pl.DeviceIdType.MESH
HBM = pl.BlockSpec(memory_space=pl.ANY)

N_ROW = 8
N_COL = 32
RING_Y = 4
RING_Z = 8
FIELDS = 4
NX = 1536
NY = 768
TURBINES = 400
BLOCKS = 48
SAMPLES = 256
LANES = 128
CT_HALF = 2.0 / 3.0
BUOYANCY = 0.3

ROWS = 768
PLANE = ROWS // FIELDS
PIECE = 2 * ROWS // N_COL
HALF = NX // 2
CHUNK = 256
CHUNKS = HALF // CHUNK
PENCIL = N_COL * PIECE
ROTOR_LINES = 16
ROTOR_TILES = NX // LANES
TURBINE_LANES = 512
BAND = 8 * PIECE


def spectral_row(length):
    offset = np.arange(length, dtype=np.int32)
    phase_angle = offset.astype(np.float32) * np.float32(np.pi / length)
    parity = np.float32(1.0) - np.float32(2.0) * (offset % 2).astype(np.float32)
    sine_safe = np.where(offset == 0, np.float32(1.0), np.sin(phase_angle))
    entries = np.float32(-(np.pi / length)) * parity * np.cos(phase_angle) / sine_safe
    entries = np.where(offset == 0, np.float32(0.0), entries)
    return entries.astype(ml_dtypes.bfloat16).astype(np.float32)


def band_x():
    m, i = np.arange(LANES)[:, None], np.arange(2 * NX)[None, :]
    return spectral_row(NX)[(m - i) % NX]


def band_y():
    depth = NY // N_COL
    r, s = np.arange(BAND)[:, None], np.arange(2 * PENCIL - BAND)[None, :] % PENCIL
    offset = (s // PIECE - r // PIECE) * depth + s % depth - r % depth
    same_level = (s % PIECE) // depth == (r % PIECE) // depth
    return np.where(same_level, spectral_row(NY)[offset % NY], np.float32(0.0))


def iota(shape, dim):
    return lax.broadcasted_iota(jnp.int32, shape, dim)


def split_points(points):
    line = ((points >> 9) * 43) >> 7
    tile = (points >> 7) - line * ROTOR_TILES
    return tile * ROTOR_LINES + line, points & (LANES - 1)


def kernel(
    fields, points, weights, turbines, counts, wide_x, wide_y,
    out, thrust_out,
    held, there, sent, back, stage_x, stage_y, tab_x, tab_y, advect, result,
    pts, wts, trb, cnt, sampled, picked, forced, push, own, from_row, from_y, from_z,
    local_sem, there_send, there_recv, back_send, back_recv, sum_send, sum_recv, out_sem,
):
    row = lax.axis_index("row")
    me = lax.axis_index("col")
    my_piece, my_half = me // 2, me % 2

    loads = [
        pltpu.make_async_copy(src, dst, local_sem.at[i])
        for i, (src, dst) in enumerate(
            [(fields, held), (points, pts), (weights, wts), (turbines, trb), (counts, cnt),
             (wide_x, stage_x), (wide_y, stage_y)]
        )
    ]

    barrier = pltpu.get_barrier_semaphore()

    def greet_col(k, carry):
        peer = lax.rem(me + k, N_COL)
        pl.semaphore_signal(barrier, inc=1, device_id={"col": peer}, device_id_type=MESH)
        return carry

    def greet_row(k, carry):
        peer = lax.rem(row + k, N_ROW)
        pl.semaphore_signal(barrier, inc=1, device_id={"row": peer}, device_id_type=MESH)
        return carry

    lax.fori_loop(1, N_COL, greet_col, 0)
    lax.fori_loop(1, N_ROW, greet_row, 0)
    for load in loads:
        load.start()
    pl.semaphore_wait(barrier, N_COL - 1 + N_ROW - 1)

    def field_piece(peer, chunk):
        start = pl.multiple_of((peer % 2) * HALF + chunk * CHUNK, CHUNK)
        return fields.at[pl.ds((peer // 2) * PIECE, PIECE), pl.ds(start, CHUNK)]

    for chunk in range(CHUNKS):

        def send_there(k, carry, chunk=chunk):
            peer = lax.rem(me + k, N_COL)
            pltpu.make_async_remote_copy(
                src_ref=field_piece(peer, chunk),
                dst_ref=there.at[chunk, pl.ds(me * PIECE, PIECE)],
                send_sem=there_send.at[chunk],
                recv_sem=there_recv.at[chunk],
                device_id={"col": peer},
                device_id_type=MESH,
            ).start()
            return carry

        lax.fori_loop(1, N_COL, send_there, 0)
        pltpu.make_async_copy(
            field_piece(me, chunk), there.at[chunk, pl.ds(me * PIECE, PIECE)], there_recv.at[chunk]
        ).start()

    for load in loads[:5]:
        load.wait()
    lines = held[0:ROTOR_LINES, :].astype(jnp.float32)
    tiles = [lines[:, LANES * i : LANES * (i + 1)] for i in range(ROTOR_TILES)]
    picked[...] = jnp.concatenate(tiles, axis=0).T.astype(jnp.bfloat16)
    table_rows = ROTOR_TILES * ROTOR_LINES

    def pick(group, carry):
        for i in range(4):
            b = group * 4 + i
            high, low = split_points(pts[pl.ds(b, 1), :])
            hot = (iota((table_rows, SAMPLES), 0) == high).astype(jnp.float32).astype(jnp.bfloat16)
            columns = jnp.dot(picked[...], hot, preferred_element_type=jnp.float32)
            chosen = jnp.where(iota((LANES, SAMPLES), 0) == low, columns, 0.0)
            sampled[pl.ds(b, 1), :] = jnp.sum(chosen, axis=0, keepdims=True)
        return carry

    lax.fori_loop(0, BLOCKS // 4, pick, 0)

    count_here = jnp.sum(
        jnp.where(iota((1, N_COL), 1) == me, cnt[...], 0), axis=1, keepdims=True
    )
    active = (iota((BLOCKS, 1), 0) < count_here).astype(jnp.float32)
    weight = wts[...].astype(jnp.float32) * active
    turbine_row = trb[pl.ds(me, 1), :]
    diagonal = iota((BLOCKS, BLOCKS), 0) == iota((BLOCKS, BLOCKS), 1)
    turbine = jnp.sum(jnp.where(diagonal, turbine_row, 0), axis=1, keepdims=True)
    belongs = (iota((BLOCKS, TURBINE_LANES), 1) == turbine).astype(jnp.float32)
    moments = (
        jnp.sum(weight * sampled[...], axis=1, keepdims=True),
        jnp.sum(weight, axis=1, keepdims=True),
    )
    per_moment = TURBINE_LANES // LANES
    for m in range(2):
        partial = jnp.sum(belongs * moments[m], axis=0, keepdims=True)
        for i in range(per_moment):
            at = m * per_moment + i
            own[0, at : at + 1, :] = partial[:, LANES * i : LANES * (i + 1)]

    def share(phase, peers, slots, peer_of):
        def send(k, carry):
            pltpu.make_async_remote_copy(
                src_ref=own.at[phase],
                dst_ref=slots.at[k - 1],
                send_sem=sum_send.at[phase],
                recv_sem=sum_recv.at[phase],
                device_id=peer_of(k),
                device_id_type=MESH,
            ).start()
            return carry

        lax.fori_loop(1, peers, send, 0)

    def collect(phase, slots):
        pltpu.make_async_copy(slots, slots, sum_recv.at[phase]).wait()
        pltpu.make_async_copy(slots, slots, sum_send.at[phase]).wait()
        return own[phase] + jnp.sum(slots[...], axis=0)

    z, y = me // RING_Y, me % RING_Y
    share(0, N_ROW, from_row, lambda k: {"row": lax.rem(row + k, N_ROW)})

    loads[5].wait()
    tab_x[...] = stage_x[...].astype(jnp.bfloat16)

    def along_x(i, carry):
        columns = pl.ds(pl.multiple_of(i * CHUNK, CHUNK), CHUNK)
        slices = [
            tab_x[:, pl.ds(pl.multiple_of(i * CHUNK + NX - LANES * a, LANES), CHUNK)]
            for a in range(NX // LANES)
        ]
        table = jnp.concatenate(slices, axis=0)
        speed = held[0:PLANE, columns].astype(jnp.float32)
        for f in range(FIELDS):
            lines = pl.ds(f * PLANE, PLANE)
            slope = jnp.dot(held[lines, :], table, preferred_element_type=jnp.float32)
            terms = -(speed * slope)
            if f == 2:
                heat = held[3 * PLANE : 4 * PLANE, columns].astype(jnp.float32)
                terms = terms + BUOYANCY * heat
            advect[lines, columns] = terms
        return carry

    lax.fori_loop(0, NX // CHUNK, along_x, 0)

    own[1] = collect(0, from_row)
    share(1, RING_Y, from_y, lambda k: {"col": z * RING_Y + lax.rem(y + k, RING_Y)})
    loads[6].wait()
    for i in range(8):
        lines = slice(i * PIECE, (i + 1) * PIECE)
        tab_y[lines, :] = stage_y[lines, :].astype(jnp.bfloat16)

    def along_y(chunk):
        pltpu.make_async_copy(there.at[chunk], there.at[chunk], there_recv.at[chunk]).wait()

        def tile(i, carry):
            start = pl.multiple_of(i * BAND, BAND)
            table = tab_y[:, pl.ds(pl.multiple_of((PENCIL - start) % PENCIL, BAND), PENCIL)]
            slope = jnp.dot(table, there[chunk], preferred_element_type=jnp.float32)
            sent[chunk, pl.ds(start, BAND), :] = slope.astype(jnp.bfloat16)
            return carry

        lax.fori_loop(0, PENCIL // BAND, tile, 0)
        landing = back.at[my_half, chunk, pl.ds(my_piece * PIECE, PIECE)]

        def send_back(k, carry):
            peer = lax.rem(me + k, N_COL)
            pltpu.make_async_remote_copy(
                src_ref=sent.at[chunk, pl.ds(peer * PIECE, PIECE)],
                dst_ref=landing,
                send_sem=back_send.at[chunk],
                recv_sem=back_recv.at[chunk],
                device_id={"col": peer},
                device_id_type=MESH,
            ).start()
            return carry

        lax.fori_loop(1, N_COL, send_back, 0)
        pltpu.make_async_copy(
            sent.at[chunk, pl.ds(me * PIECE, PIECE)], landing, back_recv.at[chunk]
        ).start()

    along_y(0)
    own[2] = collect(1, from_y)
    share(2, RING_Z, from_z, lambda k: {"col": lax.rem(z + k, RING_Z) * RING_Y + y})
    for chunk in range(1, CHUNKS):
        along_y(chunk)

    totals = collect(2, from_z)
    looked_up = []
    for m in range(2):
        parts = [totals[m * per_moment + i : m * per_moment + i + 1, :] for i in range(per_moment)]
        found = belongs * jnp.concatenate(parts, axis=1)
        looked_up.append(jnp.sum(found, axis=1, keepdims=True))
    disk_speed = looked_up[0] / (looked_up[1] + 1.0 - active)
    push[...] = -CT_HALF * (disk_speed * jnp.abs(disk_speed)) * weight
    thrust_copy = pltpu.make_async_copy(push, thrust_out, out_sem.at[2 * CHUNKS])
    thrust_copy.start()
    forced[...] = jnp.zeros_like(forced)

    def spread(group, carry):
        total = forced[...]
        for i in range(2):
            b = group * 2 + i
            high, low = split_points(pts[pl.ds(b, 1), :])
            hot = (iota((table_rows, SAMPLES), 0) == high).astype(jnp.float32).astype(jnp.bfloat16)
            value = push[pl.ds(b, 1), :]
            upper = value.astype(jnp.bfloat16).astype(jnp.float32)
            here = iota((LANES, SAMPLES), 0) == low
            placed = jnp.concatenate(
                [jnp.where(here, upper, 0.0), jnp.where(here, value - upper, 0.0)], axis=0
            ).astype(jnp.bfloat16)
            total = total + lax.dot_general(
                hot, placed, (((1,), (1,)), ((), ())), preferred_element_type=jnp.float32
            )
        forced[...] = total
        return carry

    lax.fori_loop(0, BLOCKS // 2, spread, 0)
    for i in range(ROTOR_TILES):
        lines = slice(i * ROTOR_LINES, (i + 1) * ROTOR_LINES)
        columns = slice(i * LANES, (i + 1) * LANES)
        advect[0:ROTOR_LINES, columns] += forced[lines, :LANES] + forced[lines, LANES:]

    stores = []
    for chunk in range(CHUNKS):
        pltpu.make_async_copy(back.at[:, chunk], back.at[:, chunk], back_recv.at[chunk]).wait()
        for half in range(2):
            columns = pl.ds(half * HALF + chunk * CHUNK, CHUNK)
            across = held[PLANE : 2 * PLANE, columns].astype(jnp.float32)
            for f in range(FIELDS):
                lines = pl.ds(f * PLANE, PLANE)
                term = across * back[half, chunk, lines, :].astype(jnp.float32)
                result[lines, columns] = (advect[lines, columns] - term).astype(jnp.bfloat16)
            store = pltpu.make_async_copy(
                result.at[:, columns], out.at[:, columns], out_sem.at[2 * chunk + half]
            )
            store.start()
            stores.append(store)

    for chunk in range(CHUNKS):
        others = pl.ds(0, PENCIL - PIECE)
        pltpu.make_async_copy(
            there.at[chunk, others], there.at[chunk, others], there_send.at[chunk]
        ).wait()
        pltpu.make_async_copy(
            sent.at[chunk, others], sent.at[chunk, others], back_send.at[chunk]
        ).wait()
    for store in stores:
        store.wait()
    thrust_copy.wait()


def per_device(fields, block_points, sample_weight, block_turbine, block_count):
    bf16, f32, i32 = jnp.bfloat16, jnp.float32, jnp.int32
    dma = pltpu.SemaphoreType.DMA
    tendency, thrust = pl.pallas_call(
        kernel,
        out_shape=(
            jax.ShapeDtypeStruct((ROWS, NX), bf16),
            jax.ShapeDtypeStruct((BLOCKS, SAMPLES), f32),
        ),
        in_specs=[HBM] * 7,
        out_specs=(HBM, HBM),
        scratch_shapes=[
            pltpu.VMEM((ROWS, NX), bf16),
            pltpu.VMEM((CHUNKS, PENCIL, CHUNK), bf16),
            pltpu.VMEM((CHUNKS, PENCIL, CHUNK), bf16),
            pltpu.VMEM((2, CHUNKS, ROWS, CHUNK), bf16),
            pltpu.VMEM((LANES, 2 * NX), f32),
            pltpu.VMEM((BAND, 2 * PENCIL - BAND), f32),
            pltpu.VMEM((LANES, 2 * NX), bf16),
            pltpu.VMEM((BAND, 2 * PENCIL - BAND), bf16),
            pltpu.VMEM((ROWS, NX), f32),
            pltpu.VMEM((ROWS, NX), bf16),
            pltpu.VMEM((BLOCKS, SAMPLES), i32),
            pltpu.VMEM((BLOCKS, SAMPLES), bf16),
            pltpu.VMEM((N_COL, BLOCKS), i32),
            pltpu.VMEM((1, N_COL), i32),
            pltpu.VMEM((BLOCKS, SAMPLES), f32),
            pltpu.VMEM((LANES, ROTOR_TILES * ROTOR_LINES), bf16),
            pltpu.VMEM((ROTOR_TILES * ROTOR_LINES, 2 * LANES), f32),
            pltpu.VMEM((BLOCKS, SAMPLES), f32),
            pltpu.VMEM((3, 8, LANES), f32),
            pltpu.VMEM((N_ROW - 1, 8, LANES), f32),
            pltpu.VMEM((RING_Y - 1, 8, LANES), f32),
            pltpu.VMEM((RING_Z - 1, 8, LANES), f32),
            dma((7,)),
            dma((CHUNKS,)),
            dma((CHUNKS,)),
            dma((CHUNKS,)),
            dma((CHUNKS,)),
            dma((3,)),
            dma((3,)),
            dma((2 * CHUNKS + 1,)),
        ],
        compiler_params=pltpu.CompilerParams(
            collective_id=0, has_side_effects=True, vmem_limit_bytes=56 * 2**20
        ),
        name="advection",
    )(
        fields.reshape(ROWS, NX),
        block_points.reshape(BLOCKS, SAMPLES),
        sample_weight.reshape(BLOCKS, SAMPLES),
        block_turbine.reshape(N_COL, BLOCKS),
        block_count,
        jnp.asarray(band_x()),
        jnp.asarray(band_y()),
    )
    return tendency.reshape(fields.shape), thrust.reshape(block_points.shape)


def solution(mesh):
    placed = (
        P(None, "row", "col", None),
        P("row", "col", None, None),
        P("row", "col", None, None),
        P("row", None, None),
        P("row", None),
    )
    return jax.shard_map(
        per_device,
        mesh=mesh,
        in_specs=placed,
        out_specs=(P(None, "row", "col", None), P("row", "col", None, None)),
        check_vma=False,
    )
```

time: 409 us -> 120 us (0.29)
  the two profiles are of different devices: /device:TPU:8 before, /device:TPU:64 now
where the time goes in v1:
time: 120 us; the launch traced here: 119 us
  Pallas kernels  114 us (95%)
  local copies, waits for them, and re-layouts  3.92 us (3%)
    pallas_call x1, Pallas kernels, per_device(): pl.pallas_call(kernel, out_shape=(jax.ShapeDtypeStruct((ROWS, NX), bf16),...  114 us
    unnamed x4, local copies, waits for them, and re-layouts  3.92 us

profile of v1, /device:TPU:64, one launch (start us, length us, event | category | flops | bytes accessed | tf_op | source)
XLA Modules:
  0.0 118.9 jit_solution(5556005109373810659)
XLA Ops:
  0.6 114.3 %advection.1 = (bf16[768,1536]{1,0:T(8,128)(2,1)}, f32[48,256]{1,0:T(8,128)}) custom-call(bf16[768,1536]{1,0:T(8,128)(2,1)} %bitcast.6, s32[48,256]{1,0:T(8,128)} %bitcast.8, bf16[48,256]{1,0:T(8,128)(2,1)} %bitcast.10, s32[32,48]{1,0:T(8,128)} %bitcast.11, s32[1,32]{1,0:T(1,128)} %counts.1, f32[128,3072]{1,0:T(8,128)} %constant.4.clone.wide_x, ...), custom_call_target="tpu_custom_call" | custom-call | tf_op jit(solution)/shard_map/advection/pallas_call | solution.py:330
  114.9 0.0 copy-start
  114.9 3.3 %copy.11 = bf16[4,8,24,1536]{3,2,1,0:T(8,128)(2,1)} copy(bf16[4,8,24,1536]{3,2,1,0:T(8,128)(2,1)} %bitcast.7) | data formatting | bytes 4718592
  118.2 0.0 copy-done
  118.2 0.6 copy.12
Async XLA Ops:
  114.9 3.3 %copy-start = (f32[48,256]{1,0:T(8,128)S(1)}, f32[48,256]{1,0:T(8,128)}, u32[]{:S(2)}) copy-start(f32[48,256]{1,0:T(8,128)} %get-tuple-element.5) | copy-start | bytes 147460

commit v2 on v1

--- a/solution.py
+++ b/solution.py
@@ -10,7 +10,8 @@
 from jax.sharding import PartitionSpec as P
 
 MESH = pl.DeviceIdType.MESH
-HBM = pl.BlockSpec(memory_space=pl.ANY)
+HBM = pl.BlockSpec(memory_space=pltpu.HBM)
+VMEM = pl.BlockSpec(memory_space=pltpu.VMEM)
 
 N_ROW = 8
 N_COL = 32
@@ -74,10 +75,10 @@
 
 def kernel(
     fields, points, weights, turbines, counts, wide_x, wide_y,
-    out, thrust_out,
-    held, there, sent, back, stage_x, stage_y, tab_x, tab_y, advect, result,
-    pts, wts, trb, cnt, sampled, picked, forced, push, own, from_row, from_y, from_z,
-    local_sem, there_send, there_recv, back_send, back_recv, sum_send, sum_recv, out_sem,
+    held, last_back, advect, result, push,
+    there, sent, back, stage_x, stage_y, tab_x, tab_y,
+    pts, wts, trb, cnt, sampled, picked, forced, own, from_row, from_y, from_z,
+    local_sem, there_send, there_recv, back_send, back_recv, sum_send, sum_recv,
 ):
     row = lax.axis_index("row")
     me = lax.axis_index("col")
@@ -234,7 +235,11 @@
             return carry
 
         lax.fori_loop(0, PENCIL // BAND, tile, 0)
-        landing = back.at[my_half, chunk, pl.ds(my_piece * PIECE, PIECE)]
+        lines = pl.ds(my_piece * PIECE, PIECE)
+        if chunk < CHUNKS - 1:
+            landing = back.at[my_half, chunk, lines]
+        else:
+            landing = last_back.at[my_half, lines]
 
         def send_back(k, carry):
             peer = lax.rem(me + k, N_COL)
@@ -267,8 +272,6 @@
         looked_up.append(jnp.sum(found, axis=1, keepdims=True))
     disk_speed = looked_up[0] / (looked_up[1] + 1.0 - active)
     push[...] = -CT_HALF * (disk_speed * jnp.abs(disk_speed)) * weight
-    thrust_copy = pltpu.make_async_copy(push, thrust_out, out_sem.at[2 * CHUNKS])
-    thrust_copy.start()
     forced[...] = jnp.zeros_like(forced)
 
     def spread(group, carry):
@@ -295,21 +298,12 @@
         columns = slice(i * LANES, (i + 1) * LANES)
         advect[0:ROTOR_LINES, columns] += forced[lines, :LANES] + forced[lines, LANES:]
 
-    stores = []
     for chunk in range(CHUNKS):
-        pltpu.make_async_copy(back.at[:, chunk], back.at[:, chunk], back_recv.at[chunk]).wait()
-        for half in range(2):
-            columns = pl.ds(half * HALF + chunk * CHUNK, CHUNK)
-            across = held[PLANE : 2 * PLANE, columns].astype(jnp.float32)
-            for f in range(FIELDS):
-                lines = pl.ds(f * PLANE, PLANE)
-                term = across * back[half, chunk, lines, :].astype(jnp.float32)
-                result[lines, columns] = (advect[lines, columns] - term).astype(jnp.bfloat16)
-            store = pltpu.make_async_copy(
-                result.at[:, columns], out.at[:, columns], out_sem.at[2 * chunk + half]
-            )
-            store.start()
-            stores.append(store)
+        arrived = back.at[:, chunk] if chunk < CHUNKS - 1 else last_back
+        pltpu.make_async_copy(arrived, arrived, back_recv.at[chunk]).wait()
+        if chunk < CHUNKS - 1:
+            for half in range(2):
+                combine(held, arrived.at[half], advect, result, chunk, half)
 
     for chunk in range(CHUNKS):
         others = pl.ds(0, PENCIL - PIECE)
@@ -319,33 +313,59 @@
         pltpu.make_async_copy(
             sent.at[chunk, others], sent.at[chunk, others], back_send.at[chunk]
         ).wait()
+
+
+def combine(held, arrived, advect, result, chunk, half):
+    columns = pl.ds(half * HALF + chunk * CHUNK, CHUNK)
+    across = held[PLANE : 2 * PLANE, columns].astype(jnp.float32)
+    for f in range(FIELDS):
+        lines = pl.ds(f * PLANE, PLANE)
+        term = across * arrived[lines, :].astype(jnp.float32)
+        result[lines, columns] = (advect[lines, columns] - term).astype(jnp.bfloat16)
+
+
+def finish(held, last_back, advect, result, push, out, thrust_out, merged, out_sem):
+    stores = [pltpu.make_async_copy(push, thrust_out, out_sem.at[0])]
+    for half in range(2):
+        early = pl.ds(half * HALF, HALF - CHUNK)
+        stores.append(
+            pltpu.make_async_copy(result.at[:, early], out.at[:, early], out_sem.at[1 + half])
+        )
+    for store in stores:
+        store.start()
+    for half in range(2):
+        combine(held, last_back.at[half], advect, merged, CHUNKS - 1, half)
+        late = pl.ds((half + 1) * HALF - CHUNK, CHUNK)
+        stores.append(
+            pltpu.make_async_copy(merged.at[:, late], out.at[:, late], out_sem.at[3 + half])
+        )
+        stores[-1].start()
     for store in stores:
         store.wait()
-    thrust_copy.wait()
 
 
 def per_device(fields, block_points, sample_weight, block_turbine, block_count):
     bf16, f32, i32 = jnp.bfloat16, jnp.float32, jnp.int32
     dma = pltpu.SemaphoreType.DMA
-    tendency, thrust = pl.pallas_call(
+    parts = pl.pallas_call(
         kernel,
         out_shape=(
-            jax.ShapeDtypeStruct((ROWS, NX), bf16),
-            jax.ShapeDtypeStruct((BLOCKS, SAMPLES), f32),
+            pltpu.VMEM((ROWS, NX), bf16),
+            pltpu.VMEM((2, ROWS, CHUNK), bf16),
+            pltpu.VMEM((ROWS, NX), f32),
+            pltpu.VMEM((ROWS, NX), bf16),
+            pltpu.VMEM((BLOCKS, SAMPLES), f32),
         ),
         in_specs=[HBM] * 7,
-        out_specs=(HBM, HBM),
+        out_specs=(VMEM,) * 5,
         scratch_shapes=[
-            pltpu.VMEM((ROWS, NX), bf16),
             pltpu.VMEM((CHUNKS, PENCIL, CHUNK), bf16),
             pltpu.VMEM((CHUNKS, PENCIL, CHUNK), bf16),
-            pltpu.VMEM((2, CHUNKS, ROWS, CHUNK), bf16),
+            pltpu.VMEM((2, CHUNKS - 1, ROWS, CHUNK), bf16),
             pltpu.VMEM((LANES, 2 * NX), f32),
             pltpu.VMEM((BAND, 2 * PENCIL - BAND), f32),
             pltpu.VMEM((LANES, 2 * NX), bf16),
             pltpu.VMEM((BAND, 2 * PENCIL - BAND), bf16),
-            pltpu.VMEM((ROWS, NX), f32),
-            pltpu.VMEM((ROWS, NX), bf16),
             pltpu.VMEM((BLOCKS, SAMPLES), i32),
             pltpu.VMEM((BLOCKS, SAMPLES), bf16),
             pltpu.VMEM((N_COL, BLOCKS), i32),
@@ -353,7 +373,6 @@
             pltpu.VMEM((BLOCKS, SAMPLES), f32),
             pltpu.VMEM((LANES, ROTOR_TILES * ROTOR_LINES), bf16),
             pltpu.VMEM((ROTOR_TILES * ROTOR_LINES, 2 * LANES), f32),
-            pltpu.VMEM((BLOCKS, SAMPLES), f32),
             pltpu.VMEM((3, 8, LANES), f32),
             pltpu.VMEM((N_ROW - 1, 8, LANES), f32),
             pltpu.VMEM((RING_Y - 1, 8, LANES), f32),
@@ -365,10 +384,9 @@
             dma((CHUNKS,)),
             dma((3,)),
             dma((3,)),
-            dma((2 * CHUNKS + 1,)),
         ],
         compiler_params=pltpu.CompilerParams(
-            collective_id=0, has_side_effects=True, vmem_limit_bytes=56 * 2**20
+            collective_id=0, has_side_effects=True, vmem_limit_bytes=50 * 2**20
         ),
         name="advection",
     )(
@@ -380,6 +398,18 @@
         jnp.asarray(band_x()),
         jnp.asarray(band_y()),
     )
+    tendency, thrust = pl.pallas_call(
+        finish,
+        out_shape=(
+            jax.ShapeDtypeStruct((ROWS, NX), bf16),
+            jax.ShapeDtypeStruct((BLOCKS, SAMPLES), f32),
+        ),
+        in_specs=[VMEM] * 5,
+        out_specs=(HBM, HBM),
+        scratch_shapes=[pltpu.VMEM((ROWS, NX), bf16), dma((5,))],
+        compiler_params=pltpu.CompilerParams(vmem_limit_bytes=16 * 2**20),
+        name="finish",
+    )(*parts)
     return tendency.reshape(fields.shape), thrust.reshape(block_points.shape)
 
 

time: 120 us -> 116 us (0.967)
  local copies, waits for them, and re-layouts: 3.92 us -> 0 us
    unnamed x4 -> x0, local copies, waits for them, and re-layouts: 3.92 us -> none
    pallas_call x1 -> x2, Pallas kernels: 114 us -> 115 us  [the longest x1 113 us: per_device(): pl.pallas_call(kernel, out_shape=(pltpu.VMEM((ROWS, NX), bf16), pltpu.VME...]
where the time goes in v2:
time: 116 us; the launch traced here: 115 us
  Pallas kernels  115 us (99%)
    pallas_call x1, Pallas kernels, per_device(): pl.pallas_call(kernel, out_shape=(pltpu.VMEM((ROWS, NX), bf16), pltpu.VME...  113 us

profile of v2, /device:TPU:64, one launch (start us, length us, event | category | flops | bytes accessed | tf_op | source)
XLA Modules:
  0.0 115.3 jit_solution(7005031907098873403)
XLA Ops:
  0.6 113.2 %advection.1 = (bf16[768,1536]{1,0:T(8,128)(2,1)S(1)}, bf16[2,768,256]{2,1,0:T(8,128)(2,1)S(1)}, f32[768,1536]{1,0:T(8,128)S(1)}, bf16[768,1536]{1,0:T(8,128)(2,1)S(1)}, f32[48,256]{1,0:T(8,128)S(1)}) custom-call(bf16[768,1536]{1,0:T(8,128)(2,1)} %bitcast.6, s32[48,256]{1,0:T(8,128)} %bitcast.7, bf16[48,256]{1,0:T(8,128)(2,1)} %bitcast.8, s32[32,48]{1,0:T(8,128)} %bitcast.9, ...), custom_call_target="tpu_custom_call" | custom-call | tf_op jit(solution)/shard_map/advection/pallas_call | solution.py:350
  113.8 1.5 %finish.1 = (bf16[768,1536]{1,0:T(8,128)(2,1)}, f32[48,256]{1,0:T(8,128)}) custom-call(bf16[768,1536]{1,0:T(8,128)(2,1)S(1)} %get-tuple-element.9.held, bf16[2,768,256]{2,1,0:T(8,128)(2,1)S(1)} %get-tuple-element.10.last_back, f32[768,1536]{1,0:T(8,128)S(1)} %get-tuple-element.11.advect, bf16[768,1536]{1,0:T(8,128)(2,1)S(1)} %get-tuple-element.12.result, ...), custom_call_target="tpu_custom_call" | custom-call | tf_op jit(solution)/shard_map/finish/pallas_call | solution.py:401

commit v3 on v2

--- a/solution.py
+++ b/solution.py
@@ -63,6 +63,10 @@
     return np.where(same_level, spectral_row(NY)[offset % NY], np.float32(0.0))
 
 
+def alternating(i):
+    return lax.rem(jnp.where(i % 2 == 1, (i + 1) // 2, RING_Z - i // 2), RING_Z)
+
+
 def iota(shape, dim):
     return lax.broadcasted_iota(jnp.int32, shape, dim)
 
@@ -78,7 +82,7 @@
     held, last_back, advect, result, push,
     there, sent, back, stage_x, stage_y, tab_x, tab_y,
     pts, wts, trb, cnt, sampled, picked, forced, own, from_row, from_y, from_z,
-    local_sem, there_send, there_recv, back_send, back_recv, sum_send, sum_recv,
+    local_sem, known, there_send, there_recv, back_send, back_recv, sum_send, sum_recv,
 ):
     row = lax.axis_index("row")
     me = lax.axis_index("col")
@@ -92,43 +96,71 @@
         )
     ]
 
-    barrier = pltpu.get_barrier_semaphore()
-
-    def greet_col(k, carry):
-        peer = lax.rem(me + k, N_COL)
-        pl.semaphore_signal(barrier, inc=1, device_id={"col": peer}, device_id_type=MESH)
-        return carry
+    z, y = me // RING_Y, me % RING_Y
+
+    def col_at(step_z, step_y):
+        return lax.rem(z + step_z, RING_Z) * RING_Y + lax.rem(y + step_y, RING_Y)
+
+    def greet(semaphore, steps):
+        for step in steps:
+            pl.semaphore_signal(
+                semaphore, inc=1, device_id={"col": col_at(*step)}, device_id_type=MESH
+            )
 
     def greet_row(k, carry):
         peer = lax.rem(row + k, N_ROW)
         pl.semaphore_signal(barrier, inc=1, device_id={"row": peer}, device_id_type=MESH)
         return carry
 
-    lax.fori_loop(1, N_COL, greet_col, 0)
+    def field_piece(peer, chunk):
+        start = pl.multiple_of((peer % 2) * HALF + chunk * CHUNK, CHUNK)
+        return fields.at[pl.ds((peer // 2) * PIECE, PIECE), pl.ds(start, CHUNK)]
+
+    def send_there(peer, chunk):
+        pltpu.make_async_remote_copy(
+            src_ref=field_piece(peer, chunk),
+            dst_ref=there.at[chunk, pl.ds(me * PIECE, PIECE)],
+            send_sem=there_send.at[chunk],
+            recv_sem=there_recv.at[chunk],
+            device_id={"col": peer},
+            device_id_type=MESH,
+        ).start()
+
+    barrier = pltpu.get_barrier_semaphore()
+    beside = ((1, 0), (7, 0), (0, 1), (0, 3))
+    greet(barrier, beside)
     lax.fori_loop(1, N_ROW, greet_row, 0)
     for load in loads:
         load.start()
-    pl.semaphore_wait(barrier, N_COL - 1 + N_ROW - 1)
-
-    def field_piece(peer, chunk):
-        start = pl.multiple_of((peer % 2) * HALF + chunk * CHUNK, CHUNK)
-        return fields.at[pl.ds((peer // 2) * PIECE, PIECE), pl.ds(start, CHUNK)]
-
+    pl.semaphore_wait(barrier, len(beside) + N_ROW - 1)
+    greet(known.at[0], beside)
+    for step in beside:
+        for chunk in range(CHUNKS):
+            send_there(col_at(*step), chunk)
+    pl.semaphore_wait(known.at[0], len(beside))
+    two_away = ((2, 0), (6, 0), (0, 2))
+    greet(known.at[1], two_away)
+    for step in two_away + ((1, 1), (1, 3), (7, 1), (7, 3)):
+        for chunk in range(CHUNKS):
+            send_there(col_at(*step), chunk)
+    pl.semaphore_wait(known.at[1], len(two_away))
+    greet(known.at[2], two_away[:2])
+    pl.semaphore_wait(known.at[2], 2)
     for chunk in range(CHUNKS):
 
-        def send_there(k, carry, chunk=chunk):
-            peer = lax.rem(me + k, N_COL)
-            pltpu.make_async_remote_copy(
-                src_ref=field_piece(peer, chunk),
-                dst_ref=there.at[chunk, pl.ds(me * PIECE, PIECE)],
-                send_sem=there_send.at[chunk],
-                recv_sem=there_recv.at[chunk],
-                device_id={"col": peer},
-                device_id_type=MESH,
-            ).start()
+        def send_far(i, carry, chunk=chunk):
+            far = i // RING_Y
+            send_there(col_at(jnp.where(far == 0, 4, 1 + 2 * far), i % RING_Y), chunk)
             return carry
 
-        lax.fori_loop(1, N_COL, send_there, 0)
+        def send_middle(i, carry, chunk=chunk):
+            send_there(col_at(2 + 4 * (i // 3), 1 + i % 3), chunk)
+            return carry
+
+        lax.fori_loop(0, 3 * RING_Y, send_far, 0)
+        lax.fori_loop(0, 6, send_middle, 0)
+        for step in ((1, 2), (7, 2)):
+            send_there(col_at(*step), chunk)
         pltpu.make_async_copy(
             field_piece(me, chunk), there.at[chunk, pl.ds(me * PIECE, PIECE)], there_recv.at[chunk]
         ).start()
@@ -191,7 +223,6 @@
         pltpu.make_async_copy(slots, slots, sum_send.at[phase]).wait()
         return own[phase] + jnp.sum(slots[...], axis=0)
 
-    z, y = me // RING_Y, me % RING_Y
     share(0, N_ROW, from_row, lambda k: {"row": lax.rem(row + k, N_ROW)})
 
     loads[5].wait()
@@ -242,7 +273,7 @@
             landing = last_back.at[my_half, lines]
 
         def send_back(k, carry):
-            peer = lax.rem(me + k, N_COL)
+            peer = k - 1 + (k - 1 >= me).astype(jnp.int32)
             pltpu.make_async_remote_copy(
                 src_ref=sent.at[chunk, pl.ds(peer * PIECE, PIECE)],
                 dst_ref=landing,
@@ -378,6 +409,7 @@
             pltpu.VMEM((RING_Y - 1, 8, LANES), f32),
             pltpu.VMEM((RING_Z - 1, 8, LANES), f32),
             dma((7,)),
+            pltpu.SemaphoreType.REGULAR((3,)),
             dma((CHUNKS,)),
             dma((CHUNKS,)),
             dma((CHUNKS,)),

time: 116 us -> 115 us (level)
  no operation moved by 1% of the time
where the time goes in v3:
time: 115 us
  Pallas kernels  114 us (99%)
    pallas_call x1, Pallas kernels, per_device(): pl.pallas_call(kernel, out_shape=(pltpu.VMEM((ROWS, NX), bf16), pltpu.VME...  113 us

profile of v3, /device:TPU:64, one launch (start us, length us, event | category | flops | bytes accessed | tf_op | source)
XLA Modules:
  0.0 115.1 jit_solution(7088967525828746533)
XLA Ops:
  0.6 113.0 %advection.1 = (bf16[768,1536]{1,0:T(8,128)(2,1)S(1)}, bf16[2,768,256]{2,1,0:T(8,128)(2,1)S(1)}, f32[768,1536]{1,0:T(8,128)S(1)}, bf16[768,1536]{1,0:T(8,128)(2,1)S(1)}, f32[48,256]{1,0:T(8,128)S(1)}) custom-call(bf16[768,1536]{1,0:T(8,128)(2,1)} %bitcast.6, s32[48,256]{1,0:T(8,128)} %bitcast.7, bf16[48,256]{1,0:T(8,128)(2,1)} %bitcast.8, s32[32,48]{1,0:T(8,128)} %bitcast.9, ...), custom_call_target="tpu_custom_call" | custom-call | tf_op jit(solution)/shard_map/advection/pallas_call | solution.py:381
  113.7 1.5 %finish.1 = (bf16[768,1536]{1,0:T(8,128)(2,1)}, f32[48,256]{1,0:T(8,128)}) custom-call(bf16[768,1536]{1,0:T(8,128)(2,1)S(1)} %get-tuple-element.9.held, bf16[2,768,256]{2,1,0:T(8,128)(2,1)S(1)} %get-tuple-element.10.last_back, f32[768,1536]{1,0:T(8,128)S(1)} %get-tuple-element.11.advect, bf16[768,1536]{1,0:T(8,128)(2,1)S(1)} %get-tuple-element.12.result, ...), custom_call_target="tpu_custom_call" | custom-call | tf_op jit(solution)/shard_map/finish/pallas_call | solution.py:433

commit v4 on v3

--- a/solution.py
+++ b/solution.py
@@ -38,6 +38,7 @@
 ROTOR_TILES = NX // LANES
 TURBINE_LANES = 512
 BAND = 8 * PIECE
+HUB_Z = 1
 
 
 def spectral_row(length):
@@ -81,7 +82,7 @@
     fields, points, weights, turbines, counts, wide_x, wide_y,
     held, last_back, advect, result, push,
     there, sent, back, stage_x, stage_y, tab_x, tab_y,
-    pts, wts, trb, cnt, sampled, picked, forced, own, from_row, from_y, from_z,
+    pts, wts, trb, cnt, sampled, picked, forced, own, from_row, from_y, from_z, final,
     local_sem, known, there_send, there_recv, back_send, back_recv, sum_send, sum_recv,
 ):
     row = lax.axis_index("row")
@@ -97,6 +98,8 @@
     ]
 
     z, y = me // RING_Y, me % RING_Y
+
+    hub = z == HUB_Z
 
     def col_at(step_z, step_y):
         return lax.rem(z + step_z, RING_Z) * RING_Y + lax.rem(y + step_y, RING_Y)
@@ -129,10 +132,14 @@
     barrier = pltpu.get_barrier_semaphore()
     beside = ((1, 0), (7, 0), (0, 1), (0, 3))
     greet(barrier, beside)
-    lax.fori_loop(1, N_ROW, greet_row, 0)
+
+    @pl.when(hub)
+    def _():
+        lax.fori_loop(1, N_ROW, greet_row, 0)
+
     for load in loads:
         load.start()
-    pl.semaphore_wait(barrier, len(beside) + N_ROW - 1)
+    pl.semaphore_wait(barrier, len(beside) + jnp.where(hub, N_ROW - 1, 0))
     greet(known.at[0], beside)
     for step in beside:
         for chunk in range(CHUNKS):
@@ -146,14 +153,13 @@
     pl.semaphore_wait(known.at[1], len(two_away))
     greet(known.at[2], two_away[:2])
     pl.semaphore_wait(known.at[2], 2)
-    for chunk in range(CHUNKS):
-
-        def send_far(i, carry, chunk=chunk):
+    def send_rest(chunk):
+        def send_far(i, carry):
             far = i // RING_Y
             send_there(col_at(jnp.where(far == 0, 4, 1 + 2 * far), i % RING_Y), chunk)
             return carry
 
-        def send_middle(i, carry, chunk=chunk):
+        def send_middle(i, carry):
             send_there(col_at(2 + 4 * (i // 3), 1 + i % 3), chunk)
             return carry
 
@@ -164,6 +170,8 @@
         pltpu.make_async_copy(
             field_piece(me, chunk), there.at[chunk, pl.ds(me * PIECE, PIECE)], there_recv.at[chunk]
         ).start()
+
+    send_rest(0)
 
     for load in loads[:5]:
         load.wait()
@@ -204,26 +212,25 @@
             at = m * per_moment + i
             own[0, at : at + 1, :] = partial[:, LANES * i : LANES * (i + 1)]
 
-    def share(phase, peers, slots, peer_of):
-        def send(k, carry):
-            pltpu.make_async_remote_copy(
-                src_ref=own.at[phase],
-                dst_ref=slots.at[k - 1],
-                send_sem=sum_send.at[phase],
-                recv_sem=sum_recv.at[phase],
-                device_id=peer_of(k),
-                device_id_type=MESH,
-            ).start()
-            return carry
-
-        lax.fori_loop(1, peers, send, 0)
-
-    def collect(phase, slots):
+    def tell(phase, source, slot, device):
+        pltpu.make_async_remote_copy(
+            src_ref=source,
+            dst_ref=slot,
+            send_sem=sum_send.at[phase],
+            recv_sem=sum_recv.at[phase],
+            device_id=device,
+            device_id_type=MESH,
+        ).start()
+
+    def heard(phase, slots):
         pltpu.make_async_copy(slots, slots, sum_recv.at[phase]).wait()
+
+    def told(phase, slots):
         pltpu.make_async_copy(slots, slots, sum_send.at[phase]).wait()
-        return own[phase] + jnp.sum(slots[...], axis=0)
-
-    share(0, N_ROW, from_row, lambda k: {"row": lax.rem(row + k, N_ROW)})
+
+    for k in range(1, RING_Y):
+        tell(0, own.at[0], from_y.at[k - 1], {"col": col_at(0, k)})
+    send_rest(1)
 
     loads[5].wait()
     tab_x[...] = stage_x[...].astype(jnp.bfloat16)
@@ -248,8 +255,15 @@
 
     lax.fori_loop(0, NX // CHUNK, along_x, 0)
 
-    own[1] = collect(0, from_row)
-    share(1, RING_Y, from_y, lambda k: {"col": z * RING_Y + lax.rem(y + k, RING_Y)})
+    heard(0, from_y)
+    own[1] = own[0] + jnp.sum(from_y[...], axis=0)
+
+    @pl.when(z != HUB_Z)
+    def _():
+        slot = z - (z > HUB_Z).astype(jnp.int32)
+        tell(1, own.at[1], from_z.at[slot], {"col": HUB_Z * RING_Y + y})
+
+    send_rest(2)
     loads[6].wait()
     for i in range(8):
         lines = slice(i * PIECE, (i + 1) * PIECE)
@@ -289,13 +303,25 @@
             sent.at[chunk, pl.ds(me * PIECE, PIECE)], landing, back_recv.at[chunk]
         ).start()
 
-    along_y(0)
-    own[2] = collect(1, from_y)
-    share(2, RING_Z, from_z, lambda k: {"col": lax.rem(z + k, RING_Z) * RING_Y + y})
-    for chunk in range(1, CHUNKS):
+    @pl.when(hub)
+    def _():
+        heard(1, from_z)
+        own[2] = own[1] + jnp.sum(from_z[...], axis=0)
+        for k in range(1, N_ROW):
+            tell(2, own.at[2], from_row.at[k - 1], {"row": lax.rem(row + k, N_ROW)})
+        heard(2, from_row)
+        final[...] = own[2] + jnp.sum(from_row[...], axis=0)
+        for k in range(1, RING_Z):
+            tell(3, final, final, {"col": col_at(k, 0)})
+
+    for chunk in range(CHUNKS):
         along_y(chunk)
 
-    totals = collect(2, from_z)
+    @pl.when(z != HUB_Z)
+    def _():
+        heard(3, final)
+
+    totals = final[...]
     looked_up = []
     for m in range(2):
         parts = [totals[m * per_moment + i : m * per_moment + i + 1, :] for i in range(per_moment)]
@@ -328,6 +354,17 @@
         lines = slice(i * ROTOR_LINES, (i + 1) * ROTOR_LINES)
         columns = slice(i * LANES, (i + 1) * LANES)
         advect[0:ROTOR_LINES, columns] += forced[lines, :LANES] + forced[lines, LANES:]
+
+    told(0, from_y)
+
+    @pl.when(z != HUB_Z)
+    def _():
+        told(1, from_z.at[0])
+
+    @pl.when(hub)
+    def _():
+        told(2, from_row)
+        told(3, from_z)
 
     for chunk in range(CHUNKS):
         arrived = back.at[:, chunk] if chunk < CHUNKS - 1 else last_back
@@ -408,14 +445,15 @@
             pltpu.VMEM((N_ROW - 1, 8, LANES), f32),
             pltpu.VMEM((RING_Y - 1, 8, LANES), f32),
             pltpu.VMEM((RING_Z - 1, 8, LANES), f32),
+            pltpu.VMEM((8, LANES), f32),
             dma((7,)),
             pltpu.SemaphoreType.REGULAR((3,)),
             dma((CHUNKS,)),
             dma((CHUNKS,)),
             dma((CHUNKS,)),
             dma((CHUNKS,)),
-            dma((3,)),
-            dma((3,)),
+            dma((4,)),
+            dma((4,)),
         ],
         compiler_params=pltpu.CompilerParams(
             collective_id=0, has_side_effects=True, vmem_limit_bytes=50 * 2**20

time: 115 us -> 113 us (0.983)
  Pallas kernels: 114 us -> 112 us
    pallas_call x1, Pallas kernels: 113 us -> 111 us  [per_device(): pl.pallas_call(kernel, out_shape=(pltpu.VMEM((ROWS, NX), bf16), pltpu.VME...]
where the time goes in v4:
time: 113 us
  Pallas kernels  112 us (99%)
    pallas_call x1, Pallas kernels, per_device(): pl.pallas_call(kernel, out_shape=(pltpu.VMEM((ROWS, NX), bf16), pltpu.VME...  111 us

profile of v4, /device:TPU:64, one launch (start us, length us, event | category | flops | bytes accessed | tf_op | source)
XLA Modules:
  0.0 112.7 jit_solution(4894194090252184978)
XLA Ops:
  0.6 110.6 %advection.1 = (bf16[768,1536]{1,0:T(8,128)(2,1)S(1)}, bf16[2,768,256]{2,1,0:T(8,128)(2,1)S(1)}, f32[768,1536]{1,0:T(8,128)S(1)}, bf16[768,1536]{1,0:T(8,128)(2,1)S(1)}, f32[48,256]{1,0:T(8,128)S(1)}) custom-call(bf16[768,1536]{1,0:T(8,128)(2,1)} %bitcast.6, s32[48,256]{1,0:T(8,128)} %bitcast.7, bf16[48,256]{1,0:T(8,128)(2,1)} %bitcast.8, s32[32,48]{1,0:T(8,128)} %bitcast.9, ...), custom_call_target="tpu_custom_call" | custom-call | tf_op jit(solution)/shard_map/advection/pallas_call | solution.py:418
  111.2 1.5 %finish.1 = (bf16[768,1536]{1,0:T(8,128)(2,1)}, f32[48,256]{1,0:T(8,128)}) custom-call(bf16[768,1536]{1,0:T(8,128)(2,1)S(1)} %get-tuple-element.9.held, bf16[2,768,256]{2,1,0:T(8,128)(2,1)S(1)} %get-tuple-element.10.last_back, f32[768,1536]{1,0:T(8,128)S(1)} %get-tuple-element.11.advect, bf16[768,1536]{1,0:T(8,128)(2,1)S(1)} %get-tuple-element.12.result, ...), custom_call_target="tpu_custom_call" | custom-call | tf_op jit(solution)/shard_map/finish/pallas_call | solution.py:471

commit v5 on v4

--- a/solution.py
+++ b/solution.py
@@ -287,7 +287,13 @@
             landing = last_back.at[my_half, lines]
 
         def send_back(k, carry):
-            peer = k - 1 + (k - 1 >= me).astype(jnp.int32)
+            shifted = row % 2 == 1
+            rank = jnp.where(z == 2, 0, jnp.where(z < 2, z + 1, z))
+            own_place = jnp.where(shifted, rank, z) * RING_Y + y
+            place = k - 1 + (k - 1 >= own_place).astype(jnp.int32)
+            group = place // RING_Y
+            moved = jnp.where(group == 0, 2, jnp.where(group <= 2, group - 1, group))
+            peer = jnp.where(shifted, moved, group) * RING_Y + place % RING_Y
             pltpu.make_async_remote_copy(
                 src_ref=sent.at[chunk, pl.ds(peer * PIECE, PIECE)],
                 dst_ref=landing,
@@ -366,21 +372,24 @@
         told(2, from_row)
         told(3, from_z)
 
+    def wait_sends():
+        for chunk in range(CHUNKS):
+            others = pl.ds(0, PENCIL - PIECE)
+            pltpu.make_async_copy(
+                there.at[chunk, others], there.at[chunk, others], there_send.at[chunk]
+            ).wait()
+            pltpu.make_async_copy(
+                sent.at[chunk, others], sent.at[chunk, others], back_send.at[chunk]
+            ).wait()
+
     for chunk in range(CHUNKS):
+        if chunk == CHUNKS - 1:
+            wait_sends()
         arrived = back.at[:, chunk] if chunk < CHUNKS - 1 else last_back
         pltpu.make_async_copy(arrived, arrived, back_recv.at[chunk]).wait()
         if chunk < CHUNKS - 1:
             for half in range(2):
                 combine(held, arrived.at[half], advect, result, chunk, half)
-
-    for chunk in range(CHUNKS):
-        others = pl.ds(0, PENCIL - PIECE)
-        pltpu.make_async_copy(
-            there.at[chunk, others], there.at[chunk, others], there_send.at[chunk]
-        ).wait()
-        pltpu.make_async_copy(
-            sent.at[chunk, others], sent.at[chunk, others], back_send.at[chunk]
-        ).wait()
 
 
 def combine(held, arrived, advect, result, chunk, half):

time: 113 us -> 113 us (level)
  no operation moved by 1% of the time
where the time goes in v5:
time: 113 us
  Pallas kernels  112 us (99%)
    pallas_call x1, Pallas kernels, per_device(): pl.pallas_call(kernel, out_shape=(pltpu.VMEM((ROWS, NX), bf16), pltpu.VME...  111 us

profile of v5, /device:TPU:64, one launch (start us, length us, event | category | flops | bytes accessed | tf_op | source)
XLA Modules:
  0.0 112.7 jit_solution(3502230567852683849)
XLA Ops:
  0.6 110.6 %advection.1 = (bf16[768,1536]{1,0:T(8,128)(2,1)S(1)}, bf16[2,768,256]{2,1,0:T(8,128)(2,1)S(1)}, f32[768,1536]{1,0:T(8,128)S(1)}, bf16[768,1536]{1,0:T(8,128)(2,1)S(1)}, f32[48,256]{1,0:T(8,128)S(1)}) custom-call(bf16[768,1536]{1,0:T(8,128)(2,1)} %bitcast.6, s32[48,256]{1,0:T(8,128)} %bitcast.7, bf16[48,256]{1,0:T(8,128)(2,1)} %bitcast.8, s32[32,48]{1,0:T(8,128)} %bitcast.9, ...), custom_call_target="tpu_custom_call" | custom-call | tf_op jit(solution)/shard_map/advection/pallas_call | solution.py:427
  111.2 1.5 %finish.1 = (bf16[768,1536]{1,0:T(8,128)(2,1)}, f32[48,256]{1,0:T(8,128)}) custom-call(bf16[768,1536]{1,0:T(8,128)(2,1)S(1)} %get-tuple-element.9.held, bf16[2,768,256]{2,1,0:T(8,128)(2,1)S(1)} %get-tuple-element.10.last_back, f32[768,1536]{1,0:T(8,128)S(1)} %get-tuple-element.11.advect, bf16[768,1536]{1,0:T(8,128)(2,1)S(1)} %get-tuple-element.12.result, ...), custom_call_target="tpu_custom_call" | custom-call | tf_op jit(solution)/shard_map/finish/pallas_call | solution.py:480
